TPU v7x, 512 devices: a whole 4x8x8 slice. The times are simulated.
512 devices in a mesh: space: 32 (over z_lo, y, core), mode: 16 (over z_hi, x).
Axes of the slice: x: 4, y: 8, z: 8 (z_hi: 4, z_lo: 2; z = z_hi * 2 + z_lo), core: 2. Of those that a mesh axis runs over, the one named last changes fastest.
Arguments:
- occupation_deviation: float32 [2048, 64, 4, 128], P('mode', 'space'), may hold values from -6 to 6
- initial_thermal_offset: float32 [64, 4, 128], P('space'), may hold values from -6 to 6
- branch_specific_warmth: float32 [2048], replicated, may hold values from 0.2 to 2
- courant_numbers: float32 [3, 2048], P(None, 'mode'), may hold values from 0.02 to 0.3
- sign_quadrant: int32 [2048], P('mode'), may hold values from 0 to 7
- scattering_matrix: bfloat16 [2048, 2048], P('mode'), may hold values from -1 to 1
Outputs:
- population_out: float32 [2048, 64, 4, 128], P('mode', 'space')
- thermal_offset: float32 [64, 4, 128], P('space')
All inputs are finite; a program needn't handle non-finite values.
Results may differ from a plain program's by a relative error of at most 0.002.
Values may be sent and summed in bfloat16 or wider, within the bound.
A program may use at most 64 MiB of HBM per device.

v0:
```python
import jax
import jax.numpy as jnp
from jax import lax
from jax.sharding import PartitionSpec as P

ITERS = 3


def padded_2(cells, sides, width):
    for axis, dim in sides:
        count = lax.axis_size(axis)
        head = lax.slice_in_dim(cells, 0, width, axis=dim)
        tail = lax.slice_in_dim(cells, cells.shape[dim] - width, cells.shape[dim], axis=dim)
        cells = jnp.concatenate(
            [
                lax.ppermute(tail, axis, [(i, (i + 1) % count) for i in range(count)]),
                cells,
                lax.ppermute(head, axis, [((i + 1) % count, i) for i in range(count)]),
            ],
            axis=dim,
        )
    return cells


def copy_for_each(x, axis):
    length = lax.axis_size(axis)
    return lax.all_to_all(jnp.broadcast_to(x[None], (length, *x.shape)), axis, 0, 0, tiled=True)


def joined_along(blocks, dim):
    shape = list(blocks.shape[1:])
    shape[dim] *= blocks.shape[0]
    return jnp.moveaxis(blocks, 0, dim).reshape(shape)


def gather_directly(x, axis, dim):
    blocks = copy_for_each(x, axis)
    return joined_along(blocks, dim)


def advect(lattice_wave_carry, courant_numbers, sign_quadrant):
    padded = padded_2(lattice_wave_carry, (("space", 1),), 1)
    advected = lattice_wave_carry
    for dim_index in range(3):
        if dim_index == 0:
            below_side = padded[:, :-2]
            above_side = padded[:, 2:]
        else:
            below_side = jnp.roll(lattice_wave_carry, 1, dim_index + 1)
            above_side = jnp.roll(lattice_wave_carry, -1, dim_index + 1)
        sign_bit = (sign_quadrant >> dim_index & 1).reshape(-1, 1, 1, 1)
        upwind = jnp.where(sign_bit == 1, above_side, below_side)
        advected = advected - courant_numbers[dim_index].reshape(-1, 1, 1, 1) * (
            lattice_wave_carry - upwind
        )
    return advected


def shards(
    occupation_deviation,
    initial_thermal_offset,
    branch_specific_warmth,
    courant_numbers,
    sign_quadrant,
    scattering_matrix,
):
    local_modes = occupation_deviation.shape[0]
    partition_extents = occupation_deviation.shape
    cell_count = partition_extents[1] * partition_extents[2] * partition_extents[3]
    first_mode = lax.axis_index("mode") * local_modes
    device_specific_warmth = lax.dynamic_slice_in_dim(
        branch_specific_warmth, first_mode, local_modes
    )
    summed_specific_warmth = jnp.sum(branch_specific_warmth)
    lattice_wave_carry = (
        occupation_deviation
        + device_specific_warmth.reshape(-1, 1, 1, 1) * initial_thermal_offset[None]
    )
    scattering_stripes = jnp.dot(
        scattering_matrix.astype(jnp.float32),
        branch_specific_warmth,
        precision=lax.Precision.HIGHEST,
    )
    full_matrix = lax.all_gather(scattering_matrix, "mode", axis=0, tiled=True)
    thermal_offset = jnp.zeros(partition_extents[1:], jnp.float32)
    for iteration in range(ITERS):
        upstream_occupation = advect(lattice_wave_carry, courant_numbers, sign_quadrant)
        moved_bf = upstream_occupation.astype(jnp.bfloat16)
        local_flat_bf = moved_bf.reshape(local_modes, cell_count)
        all_modes = lax.all_to_all(local_flat_bf, "mode", split_axis=1, concat_axis=0, tiled=True)
        block_product = jnp.dot(full_matrix, all_modes, preferred_element_type=jnp.float32)
        block_energy = jnp.dot(
            branch_specific_warmth, all_modes.astype(jnp.float32), precision=lax.Precision.HIGHEST
        )
        scattering_applied = lax.all_to_all(
            block_product, "mode", split_axis=0, concat_axis=1, tiled=True
        )
        internal_warmth_field = gather_directly(block_energy, "mode", 0)
        thermal_offset = (internal_warmth_field / summed_specific_warmth).reshape(
            partition_extents[1:]
        )
        lattice_wave_carry = (
            upstream_occupation
            - scattering_applied.reshape(partition_extents)
            + scattering_stripes.reshape(-1, 1, 1, 1) * thermal_offset[None]
        )
    return (lattice_wave_carry, thermal_offset)


def solution(mesh):
    placed = (
        P("mode", "space", None, None),
        P("space", None, None),
        P(),
        P(None, "mode"),
        P("mode"),
        P("mode", None),
    )
    return jax.shard_map(
        shards,
        mesh=mesh,
        in_specs=placed,
        out_specs=(P("mode", "space", None, None), P("space", None, None)),
        check_vma=False,
    )
```

profile of v0, /device:TPU:16, one launch (start us, length us, event | category | flops | bytes accessed | tf_op | source)
XLA Modules:
  0.0 312.7 jit_solution(900750973917751772)
XLA Ops:
  12.8 2.4 collective-permute-start.1
  16.9 3.6 %collective-permute-done.1 = f32[128,1,4,128]{0,3,2,1:T(8,128)S(1)} collective-permute-done((f32[128,1,4,128]{0,3,2,1:T(8,128)S(1)}, f32[128,1,4,128]{0,3,2,1:T(8,128)S(1)}, u32[]{:S(2)}, u32[]{:S(2)}) %collective-permute-start.1) | collective-permute-done | bytes 262176 | tf_op jit(solution)/shard_map/ppermute | solution.py:16
  20.8 30.4 %all_to_all.123 = bf16[128,16,64]{0,2,1:T(8,128)(2,1)S(1)} all-to-all(bf16[128,16,64]{0,2,1:T(8,128)(2,1)S(1)} %bitcast.99), channel_id=1, replica_groups=mesh['space'=32,'mode'=16] {'mode'}, dimensions={1} | all-to-all | bytes 524288 | tf_op jit(solution)/shard_map/all_to_all | solution.py:90
  52.1 6.0 %all-to-all-start.2 = ((f32[16,1,64]{2,1,0:T(1,128)}), f32[16,1,64]{2,1,0:T(1,128)S(1)}, u32[]{:S(2)}, u32[]{:S(2)}) async-start(f32[16,1,64]{2,1,0:T(1,128)} %broadcast_in_dim.58), calls=%async_computation.2 | async-start | bytes 16384 | tf_op jit(solution)/shard_map/all_to_all | solution.py:27
  58.1 86.2 %all-gather.2.cloned.1.call-done = bf16[2048,2048]{1,0:T(8,128)(2,1)} async-done(((bf16[128,2048]{1,0:T(8,128)(2,1)}), bf16[2048,2048]{1,0:T(8,128)(2,1)}) %all-gather.2.cloned.1.call-update) | async-done | bytes 8388624 | tf_op jit(solution)/shard_map/all_gather | solution.py:84
  144.3 6.0 %convolution_bitcast_fusion.2 = f32[8,16,8,128]{3,2,1,0:T(8,128)S(1)} fusion(bf16[2048,2048]{1,0:T(8,128)(2,1)} %all-gather.2.cloned.1.call-done, bf16[128,16,64]{0,2,1:T(8,128)(2,1)S(1)} %all_to_all.123), kind=kOutput, calls=%fused_computation.2 | convolution fusion | flops 536870912 | bytes 9175040 | tf_op jit(solution)/shard_map/dot_general | solution.py:91
  151.2 6.2 %all-to-all-start.1 = ((f32[16,128,64]{1,2,0:T(8,128)}), f32[16,128,64]{1,2,0:T(8,128)S(1)}, u32[]{:S(2)}, u32[]{:S(2)}) async-start(f32[16,128,64]{1,2,0:T(8,128)} %bitcast.94), calls=%async_computation.1 | async-start | bytes 1048576 | tf_op jit(solution)/shard_map/all_to_all | solution.py:95
  159.3 15.9 %all-to-all-done.1 = f32[16,128,64]{1,2,0:T(8,128)S(1)} async-done(((f32[16,128,64]{1,2,0:T(8,128)}), f32[16,128,64]{1,2,0:T(8,128)S(1)}, u32[]{:S(2)}, u32[]{:S(2)}) %all-to-all-start.1) | async-done | bytes 524320 | tf_op jit(solution)/shard_map/all_to_all | solution.py:95
  177.5 2.4 collective-permute-start.3
  181.3 3.8 %collective-permute-done.3 = f32[128,1,4,128]{0,3,2,1:T(8,128)S(1)} collective-permute-done((f32[128,1,4,128]{0,3,2,1:T(8,128)S(1)}, f32[128,1,4,128]{0,3,2,1:T(8,128)S(1)}, u32[]{:S(2)}, u32[]{:S(2)}) %collective-permute-start.3) | collective-permute-done | bytes 262176 | tf_op jit(solution)/shard_map/ppermute | solution.py:16
  185.5 16.2 %all_to_all.124 = bf16[128,16,64]{0,2,1:T(8,128)(2,1)S(1)} all-to-all(bf16[128,16,64]{0,2,1:T(8,128)(2,1)S(1)} %bitcast.100), channel_id=1, replica_groups=mesh['space'=32,'mode'=16] {'mode'}, dimensions={1} | all-to-all | bytes 524288 | tf_op jit(solution)/shard_map/all_to_all | solution.py:90
  202.6 3.8 %all-to-all-start.5 = ((f32[16,1,64]{2,1,0:T(1,128)}), f32[16,1,64]{2,1,0:T(1,128)S(1)}, u32[]{:S(2)}, u32[]{:S(2)}) async-start(f32[16,1,64]{2,1,0:T(1,128)} %broadcast_in_dim.59), calls=%async_computation.5 | async-start | bytes 16384 | tf_op jit(solution)/shard_map/all_to_all | solution.py:27
  206.4 6.0 %convolution_bitcast_fusion.1 = f32[8,16,8,128]{3,2,1,0:T(8,128)S(1)} fusion(bf16[2048,2048]{1,0:T(8,128)(2,1)} %all-gather.2.cloned.1.call-done, bf16[128,16,64]{0,2,1:T(8,128)(2,1)S(1)} %all_to_all.124), kind=kOutput, calls=%fused_computation.1 | convolution fusion | flops 536870912 | bytes 9175040 | tf_op jit(solution)/shard_map/dot_general | solution.py:91
  213.3 2.9 all-to-all-done.5
  216.2 6.7 %all-to-all-start.4 = ((f32[16,128,64]{1,2,0:T(8,128)}), f32[16,128,64]{1,2,0:T(8,128)S(1)}, u32[]{:S(2)}, u32[]{:S(2)}) async-start(f32[16,128,64]{1,2,0:T(8,128)} %bitcast.93), calls=%async_computation.4 | async-start | bytes 1048576 | tf_op jit(solution)/shard_map/all_to_all | solution.py:95
  223.6 14.6 %all-to-all-done.4 = f32[16,128,64]{1,2,0:T(8,128)S(1)} async-done(((f32[16,128,64]{1,2,0:T(8,128)}), f32[16,128,64]{1,2,0:T(8,128)S(1)}, u32[]{:S(2)}, u32[]{:S(2)}) %all-to-all-start.4) | async-done | bytes 524320 | tf_op jit(solution)/shard_map/all_to_all | solution.py:95
  240.6 2.4 collective-permute-start.5
  244.5 3.8 %collective-permute-done.5 = f32[128,1,4,128]{0,3,2,1:T(8,128)S(1)} collective-permute-done((f32[128,1,4,128]{0,3,2,1:T(8,128)S(1)}, f32[128,1,4,128]{0,3,2,1:T(8,128)S(1)}, u32[]{:S(2)}, u32[]{:S(2)}) %collective-permute-start.5) | collective-permute-done | bytes 262176 | tf_op jit(solution)/shard_map/ppermute | solution.py:16
  248.6 17.0 %all_to_all.125 = bf16[128,16,64]{0,2,1:T(8,128)(2,1)S(1)} all-to-all(bf16[128,16,64]{0,2,1:T(8,128)(2,1)S(1)} %bitcast.98), channel_id=1, replica_groups=mesh['space'=32,'mode'=16] {'mode'}, dimensions={1} | all-to-all | bytes 524288 | tf_op jit(solution)/shard_map/all_to_all | solution.py:90
  266.5 4.6 %all-to-all-start.8 = ((f32[16,1,64]{2,1,0:T(1,128)}), f32[16,1,64]{2,1,0:T(1,128)S(1)}, u32[]{:S(2)}, u32[]{:S(2)}) async-start(f32[16,1,64]{2,1,0:T(1,128)} %broadcast_in_dim.60), calls=%async_computation.8 | async-start | bytes 16384 | tf_op jit(solution)/shard_map/all_to_all | solution.py:27
  271.2 6.0 %convolution_bitcast_fusion = f32[8,16,8,128]{3,2,1,0:T(8,128)S(1)} fusion(bf16[2048,2048]{1,0:T(8,128)(2,1)} %all-gather.2.cloned.1.call-done, bf16[128,16,64]{0,2,1:T(8,128)(2,1)S(1)} %all_to_all.125), kind=kOutput, calls=%fused_computation | convolution fusion | flops 536870912 | bytes 9175040 | tf_op jit(solution)/shard_map/dot_general | solution.py:91
  278.1 2.9 all-to-all-done.8
  281.0 6.7 %all-to-all-start.7 = ((f32[16,128,64]{1,2,0:T(8,128)}), f32[16,128,64]{1,2,0:T(8,128)S(1)}, u32[]{:S(2)}, u32[]{:S(2)}) async-start(f32[16,128,64]{1,2,0:T(8,128)} %bitcast.92), calls=%async_computation.7 | async-start | bytes 1048576 | tf_op jit(solution)/shard_map/all_to_all | solution.py:95
  288.5 16.2 %all-to-all-done.7 = f32[16,128,64]{1,2,0:T(8,128)S(1)} async-done(((f32[16,128,64]{1,2,0:T(8,128)}), f32[16,128,64]{1,2,0:T(8,128)S(1)}, u32[]{:S(2)}, u32[]{:S(2)}) %all-to-all-start.7) | async-done | bytes 524320 | tf_op jit(solution)/shard_map/all_to_all | solution.py:95
  (59 shorter events, 25.6 us)
Async XLA Ops:
  7.2 44.0 %copy-start.1 = (f32[2048]{0:T(1024)S(1)}, f32[2048]{0:T(1024)}, u32[]{:S(2)}) copy-start(f32[2048]{0:T(1024)} %param.8) | copy-start | bytes 24580
  7.2 137.1 %all-gather.2.cloned.1.call-start = ((), (), s32[]{:S(2)}) async-start(), calls=%async_computation.9 | async-start | bytes 8912896 | tf_op jit(solution)/shard_map/all_gather | solution.py:84
  10.9 6.0 %collective-permute-start = (f32[128,1,4,128]{0,3,2,1:T(8,128)S(1)}, f32[128,1,4,128]{0,3,2,1:T(8,128)S(1)}, u32[]{:S(2)}, u32[]{:S(2)}) collective-permute-start(f32[128,1,4,128]{0,3,2,1:T(8,128)S(1)} %get-tuple-element.32), channel_id=1, source_target_pairs={{16,0},{32,16},{48,32},{64,48},{80,64},{96,80},{112,96},{128,112},... | collective-permute-start | bytes 786440 | tf_op jit(solution)/shard_map/ppermute | solution.py:18
  12.8 7.7 %collective-permute-start.1 = (f32[128,1,4,128]{0,3,2,1:T(8,128)S(1)}, f32[128,1,4,128]{0,3,2,1:T(8,128)S(1)}, u32[]{:S(2)}, u32[]{:S(2)}) collective-permute-start(f32[128,1,4,128]{0,3,2,1:T(8,128)S(1)} %get-tuple-element.33), channel_id=1, source_target_pairs={{0,16},{16,32},{32,48},{48,64},{64,80},{80,96},{96,112},{112,128},... | collective-permute-start | bytes 786440 | tf_op jit(solution)/shard_map/ppermute | solution.py:16
  16.9 141.1 %copy-start = (bf16[128,2048]{1,0:T(8,128)(2,1)S(1)}, bf16[128,2048]{1,0:T(8,128)(2,1)}, u32[]{:S(2)}) copy-start(bf16[128,2048]{1,0:T(8,128)(2,1)} %param.11) | copy-start | bytes 1572868
  52.1 99.1 %all-to-all-start.2 = ((f32[16,1,64]{2,1,0:T(1,128)}), f32[16,1,64]{2,1,0:T(1,128)S(1)}, u32[]{:S(2)}, u32[]{:S(2)}) async-start(f32[16,1,64]{2,1,0:T(1,128)} %broadcast_in_dim.58), calls=%async_computation.2 | async-start | bytes 16384 | tf_op jit(solution)/shard_map/all_to_all | solution.py:27
  151.2 23.9 %all-to-all-start.1 = ((f32[16,128,64]{1,2,0:T(8,128)}), f32[16,128,64]{1,2,0:T(8,128)S(1)}, u32[]{:S(2)}, u32[]{:S(2)}) async-start(f32[16,128,64]{1,2,0:T(8,128)} %bitcast.94), calls=%async_computation.1 | async-start | bytes 1048576 | tf_op jit(solution)/shard_map/all_to_all | solution.py:95
  175.5 5.8 %collective-permute-start.2 = (f32[128,1,4,128]{0,3,2,1:T(8,128)S(1)}, f32[128,1,4,128]{0,3,2,1:T(8,128)S(1)}, u32[]{:S(2)}, u32[]{:S(2)}) collective-permute-start(f32[128,1,4,128]{0,3,2,1:T(8,128)S(1)} %get-tuple-element.22), channel_id=1, source_target_pairs={{16,0},{32,16},{48,32},{64,48},{80,64},{96,80},{112,96},{128,112},... | collective-permute-start | bytes 786440 | tf_op jit(solution)/shard_map/ppermute | solution.py:18
  177.5 7.7 %collective-permute-start.3 = (f32[128,1,4,128]{0,3,2,1:T(8,128)S(1)}, f32[128,1,4,128]{0,3,2,1:T(8,128)S(1)}, u32[]{:S(2)}, u32[]{:S(2)}) collective-permute-start(f32[128,1,4,128]{0,3,2,1:T(8,128)S(1)} %get-tuple-element.23), channel_id=1, source_target_pairs={{0,16},{16,32},{32,48},{48,64},{64,80},{80,96},{96,112},{112,128},... | collective-permute-start | bytes 786440 | tf_op jit(solution)/shard_map/ppermute | solution.py:16
  202.6 13.6 %all-to-all-start.5 = ((f32[16,1,64]{2,1,0:T(1,128)}), f32[16,1,64]{2,1,0:T(1,128)S(1)}, u32[]{:S(2)}, u32[]{:S(2)}) async-start(f32[16,1,64]{2,1,0:T(1,128)} %broadcast_in_dim.59), calls=%async_computation.5 | async-start | bytes 16384 | tf_op jit(solution)/shard_map/all_to_all | solution.py:27
  216.2 22.1 %all-to-all-start.4 = ((f32[16,128,64]{1,2,0:T(8,128)}), f32[16,128,64]{1,2,0:T(8,128)S(1)}, u32[]{:S(2)}, u32[]{:S(2)}) async-start(f32[16,128,64]{1,2,0:T(8,128)} %bitcast.93), calls=%async_computation.4 | async-start | bytes 1048576 | tf_op jit(solution)/shard_map/all_to_all | solution.py:95
  238.7 5.8 %collective-permute-start.4 = (f32[128,1,4,128]{0,3,2,1:T(8,128)S(1)}, f32[128,1,4,128]{0,3,2,1:T(8,128)S(1)}, u32[]{:S(2)}, u32[]{:S(2)}) collective-permute-start(f32[128,1,4,128]{0,3,2,1:T(8,128)S(1)} %get-tuple-element.12), channel_id=1, source_target_pairs={{16,0},{32,16},{48,32},{64,48},{80,64},{96,80},{112,96},{128,112},... | collective-permute-start | bytes 786440 | tf_op jit(solution)/shard_map/ppermute | solution.py:18
  240.6 7.7 %collective-permute-start.5 = (f32[128,1,4,128]{0,3,2,1:T(8,128)S(1)}, f32[128,1,4,128]{0,3,2,1:T(8,128)S(1)}, u32[]{:S(2)}, u32[]{:S(2)}) collective-permute-start(f32[128,1,4,128]{0,3,2,1:T(8,128)S(1)} %get-tuple-element.13), channel_id=1, source_target_pairs={{0,16},{16,32},{32,48},{48,64},{64,80},{80,96},{96,112},{112,128},... | collective-permute-start | bytes 786440 | tf_op jit(solution)/shard_map/ppermute | solution.py:16
  266.5 14.5 %all-to-all-start.8 = ((f32[16,1,64]{2,1,0:T(1,128)}), f32[16,1,64]{2,1,0:T(1,128)S(1)}, u32[]{:S(2)}, u32[]{:S(2)}) async-start(f32[16,1,64]{2,1,0:T(1,128)} %broadcast_in_dim.60), calls=%async_computation.8 | async-start | bytes 16384 | tf_op jit(solution)/shard_map/all_to_all | solution.py:27
  281.0 23.6 %all-to-all-start.7 = ((f32[16,128,64]{1,2,0:T(8,128)}), f32[16,128,64]{1,2,0:T(8,128)S(1)}, u32[]{:S(2)}, u32[]{:S(2)}) async-start(f32[16,128,64]{1,2,0:T(8,128)} %bitcast.92), calls=%async_computation.7 | async-start | bytes 1048576 | tf_op jit(solution)/shard_map/all_to_all | solution.py:95
  288.5 17.4 %copy-start.2 = (f32[2,4,128]{2,1,0:T(4,128)}, f32[2,4,128]{2,1,0:T(4,128)S(1)}, u32[]{:S(2)}) copy-start(f32[2,4,128]{2,1,0:T(4,128)S(1)} %div.42) | copy-start | bytes 12292
Sparse Core Ops, SparseCore 0:
  11.0 133.2 all-gather.1
where the time goes:
time: 314 us; the launch traced here: 313 us
  waiting for transfers between devices  153 us (49%)
  blocking collectives  63.5 us (20%)
  starting transfers between devices  47 us (15%)
  matrix products  19.5 us (6%)
  between operations  14.3 us (5%)
  local copies, waits for them, and re-layouts  9.09 us (3%)
  other arithmetic  5.87 us (2%)
    all_gather x1, waiting for transfers between devices, shards(): full_matrix = lax.all_gather(scattering_matrix, 'mode', axis=0, tiled=True)  86.2 us
    all_to_all x3, blocking collectives, shards(): lax.all_to_all(local_flat_bf, 'mode', split_axis=1, concat_axis=0, tiled=...  63.5 us
    all_to_all x3, waiting for transfers between devices, shards(): lax.all_to_all(block_product, 'mode', split_axis=0, concat_axis=1, tiled=...  46.7 us
    all_to_all x3, starting transfers between devices, shards(): lax.all_to_all(block_product, 'mode', split_axis=0, concat_axis=1, tiled=...  19.6 us
    dot_general x3, matrix products, shards(): jnp.dot(full_matrix, all_modes, preferred_element_type=jnp.float32)  18.1 us
    all_to_all x3, starting transfers between devices, copy_for_each(): lax.all_to_all(jnp.broadcast_to(x[None], (length, *x.shape)), axis, 0, 0,...  14.4 us
    ppermute x3, waiting for transfers between devices, padded_2(): lax.ppermute(tail, axis, [(i, (i + 1) % count) for i in range(count)])  11.2 us
    ppermute x3, starting transfers between devices, padded_2(): lax.ppermute(tail, axis, [(i, (i + 1) % count) for i in range(count)])  7.22 us
  transfers between devices with their start and end apart: 13, of which 11 were waited for; matrix products, arithmetic and copies ran while one was open for 10% of the time, Pallas kernels for 0%

commit v1 on v0

--- a/solution.py
+++ b/solution.py
@@ -81,7 +81,10 @@
         branch_specific_warmth,
         precision=lax.Precision.HIGHEST,
     )
-    full_matrix = lax.all_gather(scattering_matrix, "mode", axis=0, tiled=True)
+    peers = lax.axis_size("mode")
+    pieces = jnp.stack([scattering_matrix for _ in range(peers)])
+    pieces = lax.all_to_all(pieces, "mode", split_axis=0, concat_axis=0)
+    full_matrix = jnp.concatenate(pieces, axis=0)
     thermal_offset = jnp.zeros(partition_extents[1:], jnp.float32)
     for iteration in range(ITERS):
         upstream_occupation = advect(lattice_wave_carry, courant_numbers, sign_quadrant)

time: 314 us -> 414 us (1.32)
  the two profiles are of different devices: /device:TPU:16 before, /device:TPU:4 now
where the time goes in v1:
time: 414 us; the launch traced here: 412 us
  waiting for transfers between devices  239 us (58%)
  starting transfers between devices  77.8 us (19%)
  blocking collectives  55.7 us (13%)
  matrix products  19.5 us (5%)
  local copies, waits for them, and re-layouts  13.4 us (3%)
  other arithmetic  5.85 us (1%)
    all_to_all x1, waiting for transfers between devices, shards(): pieces = lax.all_to_all(pieces, 'mode', split_axis=0, concat_axis=0)  184 us
    all_to_all x3, blocking collectives, shards(): lax.all_to_all(local_flat_bf, 'mode', split_axis=1, concat_axis=0, tiled=...  55.7 us
    all_to_all x3, waiting for transfers between devices, shards(): lax.all_to_all(block_product, 'mode', split_axis=0, concat_axis=1, tiled=...  30.2 us
    all_to_all x3, starting transfers between devices, shards(): lax.all_to_all(block_product, 'mode', split_axis=0, concat_axis=1, tiled=...  26.3 us
    ppermute x3, starting transfers between devices, padded_2(): lax.ppermute(head, axis, [((i + 1) % count, i) for i in range(count)])  21.1 us
    ppermute x3, waiting for transfers between devices, padded_2(): lax.ppermute(tail, axis, [(i, (i + 1) % count) for i in range(count)])  18.5 us
    dot_general x3, matrix products, shards(): jnp.dot(full_matrix, all_modes, preferred_element_type=jnp.float32)  18.1 us
    all_to_all x3, starting transfers between devices, copy_for_each(): lax.all_to_all(jnp.broadcast_to(x[None], (length, *x.shape)), axis, 0, 0,...  17.6 us
  transfers between devices with their start and end apart: 13, of which 13 were waited for; matrix products, arithmetic and copies ran while one was open for 6% of the time, Pallas kernels for 0%

profile of v1, /device:TPU:4, one launch (start us, length us, event | category | flops | bytes accessed | tf_op | source)
XLA Modules:
  0.0 412.4 jit_solution(14406199927744618353)
XLA Ops:
  3.6 6.6 %collective-permute-start = (f32[128,1,4,128]{0,3,2,1:T(8,128)S(1)}, f32[128,1,4,128]{0,3,2,1:T(8,128)S(1)}, u32[]{:S(2)}, u32[]{:S(2)}) collective-permute-start(f32[128,1,4,128]{0,3,2,1:T(8,128)S(1)} %get-tuple-element.32), channel_id=1, source_target_pairs={{16,0},{32,16},{48,32},{64,48},{80,64},{96,80},{112,96},{128,112},... | collective-permute-start | bytes 786440 | tf_op jit(solution)/shard_map/ppermute | solution.py:18
  14.1 5.9 %collective-permute-done.1 = f32[128,1,4,128]{0,3,2,1:T(8,128)S(1)} collective-permute-done((f32[128,1,4,128]{0,3,2,1:T(8,128)S(1)}, f32[128,1,4,128]{0,3,2,1:T(8,128)S(1)}, u32[]{:S(2)}, u32[]{:S(2)}) %collective-permute-start.1) | collective-permute-done | bytes 262176 | tf_op jit(solution)/shard_map/ppermute | solution.py:16
  20.4 21.5 %all_to_all.128 = bf16[128,16,64]{0,2,1:T(8,128)(2,1)S(1)} all-to-all(bf16[128,16,64]{0,2,1:T(8,128)(2,1)S(1)} %bitcast.100), channel_id=1, replica_groups=mesh['space'=32,'mode'=16] {'mode'}, dimensions={1} | all-to-all | bytes 524288 | tf_op jit(solution)/shard_map/all_to_all | solution.py:93
  41.9 4.3 %stack.2 = bf16[16,128,2048]{2,1,0:T(8,128)(2,1)} broadcast(bf16[128,2048]{1,0:T(8,128)(2,1)S(1)} %copy-done), dimensions={1,2} | broadcast | bytes 8912896 | tf_op jit(solution)/shard_map/stack | solution.py:85
  46.2 6.5 %all-to-all-start.1 = ((bf16[16,128,2048]{2,1,0:T(8,128)(2,1)}), bf16[16,128,2048]{2,1,0:T(8,128)(2,1)}, u32[]{:S(2)}, u32[]{:S(2)}) async-start(bf16[16,128,2048]{2,1,0:T(8,128)(2,1)} %stack.2), calls=%async_computation.1 | async-start | bytes 16777216 | tf_op jit(solution)/shard_map/all_to_all | solution.py:86
  53.0 184.5 %all-to-all-done.1 = bf16[16,128,2048]{2,1,0:T(8,128)(2,1)} async-done(((bf16[16,128,2048]{2,1,0:T(8,128)(2,1)}), bf16[16,128,2048]{2,1,0:T(8,128)(2,1)}, u32[]{:S(2)}, u32[]{:S(2)}) %all-to-all-start.1) | async-done | bytes 8388640 | tf_op jit(solution)/shard_map/all_to_all | solution.py:86
  238.1 7.1 %all-to-all-start.3 = ((f32[16,1,64]{2,1,0:T(1,128)}), f32[16,1,64]{2,1,0:T(1,128)S(1)}, u32[]{:S(2)}, u32[]{:S(2)}) async-start(f32[16,1,64]{2,1,0:T(1,128)} %broadcast_in_dim.58), calls=%async_computation.3 | async-start | bytes 16384 | tf_op jit(solution)/shard_map/all_to_all | solution.py:27
  245.2 6.0 %convolution_bitcast_fusion.2 = f32[8,16,8,128]{3,2,1,0:T(8,128)S(1)} fusion(bf16[2048,2048]{1,0:T(8,128)(2,1)} %bitcast.5, bf16[128,16,64]{0,2,1:T(8,128)(2,1)S(1)} %all_to_all.128), kind=kOutput, calls=%fused_computation.2 | convolution fusion | flops 536870912 | bytes 9175040 | tf_op jit(solution)/shard_map/dot_general | solution.py:94
  252.9 8.8 %all-to-all-start.2 = ((f32[16,128,64]{1,2,0:T(8,128)}), f32[16,128,64]{1,2,0:T(8,128)S(1)}, u32[]{:S(2)}, u32[]{:S(2)}) async-start(f32[16,128,64]{1,2,0:T(8,128)} %bitcast.95), calls=%async_computation.2 | async-start | bytes 1048576 | tf_op jit(solution)/shard_map/all_to_all | solution.py:98
  263.6 9.8 %all-to-all-done.2 = f32[16,128,64]{1,2,0:T(8,128)S(1)} async-done(((f32[16,128,64]{1,2,0:T(8,128)}), f32[16,128,64]{1,2,0:T(8,128)S(1)}, u32[]{:S(2)}, u32[]{:S(2)}) %all-to-all-start.2) | async-done | bytes 524320 | tf_op jit(solution)/shard_map/all_to_all | solution.py:98
  273.8 12.5 %collective-permute-start.2 = (f32[128,1,4,128]{0,3,2,1:T(8,128)S(1)}, f32[128,1,4,128]{0,3,2,1:T(8,128)S(1)}, u32[]{:S(2)}, u32[]{:S(2)}) collective-permute-start(f32[128,1,4,128]{0,3,2,1:T(8,128)S(1)} %get-tuple-element.22), channel_id=1, source_target_pairs={{16,0},{32,16},{48,32},{64,48},{80,64},{96,80},{112,96},{128,112},... | collective-permute-start | bytes 786440 | tf_op jit(solution)/shard_map/ppermute | solution.py:18
  290.2 6.6 %collective-permute-done.3 = f32[128,1,4,128]{0,3,2,1:T(8,128)S(1)} collective-permute-done((f32[128,1,4,128]{0,3,2,1:T(8,128)S(1)}, f32[128,1,4,128]{0,3,2,1:T(8,128)S(1)}, u32[]{:S(2)}, u32[]{:S(2)}) %collective-permute-start.3) | collective-permute-done | bytes 262176 | tf_op jit(solution)/shard_map/ppermute | solution.py:16
  297.1 18.4 %all_to_all.129 = bf16[128,16,64]{0,2,1:T(8,128)(2,1)S(1)} all-to-all(bf16[128,16,64]{0,2,1:T(8,128)(2,1)S(1)} %bitcast.101), channel_id=1, replica_groups=mesh['space'=32,'mode'=16] {'mode'}, dimensions={1} | all-to-all | bytes 524288 | tf_op jit(solution)/shard_map/all_to_all | solution.py:93
  316.5 5.3 %all-to-all-start.6 = ((f32[16,1,64]{2,1,0:T(1,128)}), f32[16,1,64]{2,1,0:T(1,128)S(1)}, u32[]{:S(2)}, u32[]{:S(2)}) async-start(f32[16,1,64]{2,1,0:T(1,128)} %broadcast_in_dim.59), calls=%async_computation.6 | async-start | bytes 16384 | tf_op jit(solution)/shard_map/all_to_all | solution.py:27
  321.7 6.0 %convolution_bitcast_fusion.1 = f32[8,16,8,128]{3,2,1,0:T(8,128)S(1)} fusion(bf16[2048,2048]{1,0:T(8,128)(2,1)} %bitcast.5, bf16[128,16,64]{0,2,1:T(8,128)(2,1)S(1)} %all_to_all.129), kind=kOutput, calls=%fused_computation.1 | convolution fusion | flops 536870912 | bytes 9175040 | tf_op jit(solution)/shard_map/dot_general | solution.py:94
  329.5 8.8 %all-to-all-start.5 = ((f32[16,128,64]{1,2,0:T(8,128)}), f32[16,128,64]{1,2,0:T(8,128)S(1)}, u32[]{:S(2)}, u32[]{:S(2)}) async-start(f32[16,128,64]{1,2,0:T(8,128)} %bitcast.94), calls=%async_computation.5 | async-start | bytes 1048576 | tf_op jit(solution)/shard_map/all_to_all | solution.py:98
  339.0 10.3 %all-to-all-done.5 = f32[16,128,64]{1,2,0:T(8,128)S(1)} async-done(((f32[16,128,64]{1,2,0:T(8,128)}), f32[16,128,64]{1,2,0:T(8,128)S(1)}, u32[]{:S(2)}, u32[]{:S(2)}) %all-to-all-start.5) | async-done | bytes 524320 | tf_op jit(solution)/shard_map/all_to_all | solution.py:98
  351.6 2.4 collective-permute-start.5
  355.5 5.9 %collective-permute-done.5 = f32[128,1,4,128]{0,3,2,1:T(8,128)S(1)} collective-permute-done((f32[128,1,4,128]{0,3,2,1:T(8,128)S(1)}, f32[128,1,4,128]{0,3,2,1:T(8,128)S(1)}, u32[]{:S(2)}, u32[]{:S(2)}) %collective-permute-start.5) | collective-permute-done | bytes 262176 | tf_op jit(solution)/shard_map/ppermute | solution.py:16
  361.7 15.9 %all_to_all.130 = bf16[128,16,64]{0,2,1:T(8,128)(2,1)S(1)} all-to-all(bf16[128,16,64]{0,2,1:T(8,128)(2,1)S(1)} %bitcast.99), channel_id=1, replica_groups=mesh['space'=32,'mode'=16] {'mode'}, dimensions={1} | all-to-all | bytes 524288 | tf_op jit(solution)/shard_map/all_to_all | solution.py:93
  378.5 5.3 %all-to-all-start.9 = ((f32[16,1,64]{2,1,0:T(1,128)}), f32[16,1,64]{2,1,0:T(1,128)S(1)}, u32[]{:S(2)}, u32[]{:S(2)}) async-start(f32[16,1,64]{2,1,0:T(1,128)} %broadcast_in_dim.60), calls=%async_computation.9 | async-start | bytes 16384 | tf_op jit(solution)/shard_map/all_to_all | solution.py:27
  383.8 6.0 %convolution_bitcast_fusion = f32[8,16,8,128]{3,2,1,0:T(8,128)S(1)} fusion(bf16[2048,2048]{1,0:T(8,128)(2,1)} %bitcast.5, bf16[128,16,64]{0,2,1:T(8,128)(2,1)S(1)} %all_to_all.130), kind=kOutput, calls=%fused_computation | convolution fusion | flops 536870912 | bytes 9175040 | tf_op jit(solution)/shard_map/dot_general | solution.py:94
  391.5 8.8 %all-to-all-start.8 = ((f32[16,128,64]{1,2,0:T(8,128)}), f32[16,128,64]{1,2,0:T(8,128)S(1)}, u32[]{:S(2)}, u32[]{:S(2)}) async-start(f32[16,128,64]{1,2,0:T(8,128)} %bitcast.93), calls=%async_computation.8 | async-start | bytes 1048576 | tf_op jit(solution)/shard_map/all_to_all | solution.py:98
  401.1 10.1 %all-to-all-done.8 = f32[16,128,64]{1,2,0:T(8,128)S(1)} async-done(((f32[16,128,64]{1,2,0:T(8,128)}), f32[16,128,64]{1,2,0:T(8,128)S(1)}, u32[]{:S(2)}, u32[]{:S(2)}) %all-to-all-start.8) | async-done | bytes 524320 | tf_op jit(solution)/shard_map/all_to_all | solution.py:98
  (59 shorter events, 28.2 us)
Async XLA Ops:
  0.6 41.2 %copy-start = (bf16[128,2048]{1,0:T(8,128)(2,1)S(1)}, bf16[128,2048]{1,0:T(8,128)(2,1)}, u32[]{:S(2)}) copy-start(bf16[128,2048]{1,0:T(8,128)(2,1)} %param.11) | copy-start | bytes 1572868
  3.6 10.5 %collective-permute-start = (f32[128,1,4,128]{0,3,2,1:T(8,128)S(1)}, f32[128,1,4,128]{0,3,2,1:T(8,128)S(1)}, u32[]{:S(2)}, u32[]{:S(2)}) collective-permute-start(f32[128,1,4,128]{0,3,2,1:T(8,128)S(1)} %get-tuple-element.32), channel_id=1, source_target_pairs={{16,0},{32,16},{48,32},{64,48},{80,64},{96,80},{112,96},{128,112},... | collective-permute-start | bytes 786440 | tf_op jit(solution)/shard_map/ppermute | solution.py:18
  10.3 9.8 %collective-permute-start.1 = (f32[128,1,4,128]{0,3,2,1:T(8,128)S(1)}, f32[128,1,4,128]{0,3,2,1:T(8,128)S(1)}, u32[]{:S(2)}, u32[]{:S(2)}) collective-permute-start(f32[128,1,4,128]{0,3,2,1:T(8,128)S(1)} %get-tuple-element.33), channel_id=1, source_target_pairs={{0,16},{16,32},{32,48},{48,64},{64,80},{80,96},{96,112},{112,128},... | collective-permute-start | bytes 786440 | tf_op jit(solution)/shard_map/ppermute | solution.py:16
  46.2 6.5 %copy-start.1 = (f32[2048]{0:T(1024)S(1)}, f32[2048]{0:T(1024)}, u32[]{:S(2)}) copy-start(f32[2048]{0:T(1024)} %param.8) | copy-start | bytes 24580
  46.2 191.3 %all-to-all-start.1 = ((bf16[16,128,2048]{2,1,0:T(8,128)(2,1)}), bf16[16,128,2048]{2,1,0:T(8,128)(2,1)}, u32[]{:S(2)}, u32[]{:S(2)}) async-start(bf16[16,128,2048]{2,1,0:T(8,128)(2,1)} %stack.2), calls=%async_computation.1 | async-start | bytes 16777216 | tf_op jit(solution)/shard_map/all_to_all | solution.py:86
  238.1 14.8 %all-to-all-start.3 = ((f32[16,1,64]{2,1,0:T(1,128)}), f32[16,1,64]{2,1,0:T(1,128)S(1)}, u32[]{:S(2)}, u32[]{:S(2)}) async-start(f32[16,1,64]{2,1,0:T(1,128)} %broadcast_in_dim.58), calls=%async_computation.3 | async-start | bytes 16384 | tf_op jit(solution)/shard_map/all_to_all | solution.py:27
  252.9 20.4 %all-to-all-start.2 = ((f32[16,128,64]{1,2,0:T(8,128)}), f32[16,128,64]{1,2,0:T(8,128)S(1)}, u32[]{:S(2)}, u32[]{:S(2)}) async-start(f32[16,128,64]{1,2,0:T(8,128)} %bitcast.95), calls=%async_computation.2 | async-start | bytes 1048576 | tf_op jit(solution)/shard_map/all_to_all | solution.py:98
  273.8 16.5 %collective-permute-start.2 = (f32[128,1,4,128]{0,3,2,1:T(8,128)S(1)}, f32[128,1,4,128]{0,3,2,1:T(8,128)S(1)}, u32[]{:S(2)}, u32[]{:S(2)}) collective-permute-start(f32[128,1,4,128]{0,3,2,1:T(8,128)S(1)} %get-tuple-element.22), channel_id=1, source_target_pairs={{16,0},{32,16},{48,32},{64,48},{80,64},{96,80},{112,96},{128,112},... | collective-permute-start | bytes 786440 | tf_op jit(solution)/shard_map/ppermute | solution.py:18
  286.3 10.5 %collective-permute-start.3 = (f32[128,1,4,128]{0,3,2,1:T(8,128)S(1)}, f32[128,1,4,128]{0,3,2,1:T(8,128)S(1)}, u32[]{:S(2)}, u32[]{:S(2)}) collective-permute-start(f32[128,1,4,128]{0,3,2,1:T(8,128)S(1)} %get-tuple-element.23), channel_id=1, source_target_pairs={{0,16},{16,32},{32,48},{48,64},{64,80},{80,96},{96,112},{112,128},... | collective-permute-start | bytes 786440 | tf_op jit(solution)/shard_map/ppermute | solution.py:16
  316.5 13.0 %all-to-all-start.6 = ((f32[16,1,64]{2,1,0:T(1,128)}), f32[16,1,64]{2,1,0:T(1,128)S(1)}, u32[]{:S(2)}, u32[]{:S(2)}) async-start(f32[16,1,64]{2,1,0:T(1,128)} %broadcast_in_dim.59), calls=%async_computation.6 | async-start | bytes 16384 | tf_op jit(solution)/shard_map/all_to_all | solution.py:27
  329.5 19.8 %all-to-all-start.5 = ((f32[16,128,64]{1,2,0:T(8,128)}), f32[16,128,64]{1,2,0:T(8,128)S(1)}, u32[]{:S(2)}, u32[]{:S(2)}) async-start(f32[16,128,64]{1,2,0:T(8,128)} %bitcast.94), calls=%async_computation.5 | async-start | bytes 1048576 | tf_op jit(solution)/shard_map/all_to_all | solution.py:98
  349.7 5.8 %collective-permute-start.4 = (f32[128,1,4,128]{0,3,2,1:T(8,128)S(1)}, f32[128,1,4,128]{0,3,2,1:T(8,128)S(1)}, u32[]{:S(2)}, u32[]{:S(2)}) collective-permute-start(f32[128,1,4,128]{0,3,2,1:T(8,128)S(1)} %get-tuple-element.12), channel_id=1, source_target_pairs={{16,0},{32,16},{48,32},{64,48},{80,64},{96,80},{112,96},{128,112},... | collective-permute-start | bytes 786440 | tf_op jit(solution)/shard_map/ppermute | solution.py:18
  351.6 9.8 %collective-permute-start.5 = (f32[128,1,4,128]{0,3,2,1:T(8,128)S(1)}, f32[128,1,4,128]{0,3,2,1:T(8,128)S(1)}, u32[]{:S(2)}, u32[]{:S(2)}) collective-permute-start(f32[128,1,4,128]{0,3,2,1:T(8,128)S(1)} %get-tuple-element.13), channel_id=1, source_target_pairs={{0,16},{16,32},{32,48},{48,64},{64,80},{80,96},{96,112},{112,128},... | collective-permute-start | bytes 786440 | tf_op jit(solution)/shard_map/ppermute | solution.py:16
  378.5 13.0 %all-to-all-start.9 = ((f32[16,1,64]{2,1,0:T(1,128)}), f32[16,1,64]{2,1,0:T(1,128)S(1)}, u32[]{:S(2)}, u32[]{:S(2)}) async-start(f32[16,1,64]{2,1,0:T(1,128)} %broadcast_in_dim.60), calls=%async_computation.9 | async-start | bytes 16384 | tf_op jit(solution)/shard_map/all_to_all | solution.py:27
  391.5 19.7 %all-to-all-start.8 = ((f32[16,128,64]{1,2,0:T(8,128)}), f32[16,128,64]{1,2,0:T(8,128)S(1)}, u32[]{:S(2)}, u32[]{:S(2)}) async-start(f32[16,128,64]{1,2,0:T(8,128)} %bitcast.93), calls=%async_computation.8 | async-start | bytes 1048576 | tf_op jit(solution)/shard_map/all_to_all | solution.py:98
  401.1 11.4 %copy-start.2 = (f32[2,4,128]{2,1,0:T(4,128)}, f32[2,4,128]{2,1,0:T(4,128)S(1)}, u32[]{:S(2)}) copy-start(f32[2,4,128]{2,1,0:T(4,128)S(1)} %div.42) | copy-start | bytes 12292
